TPU v7x, 32 devices: a whole 2x2x4 slice. The times are simulated.
32 devices in a mesh: lag: 2 (over y), patch: 16 (over z, x, core).
Axes of the slice: x: 2, y: 2, z: 4, core: 2. Of those that a mesh axis runs over, the one named last changes fastest.
Arguments:
- incident: bfloat16 [4, 8192, 128], P(None, 'patch'), may hold values from -6 to 6
- pending: float32 [2, 8192, 128], P('lag', 'patch'), may hold values from -6 to 6
- self_inverse: float32 [64, 128, 128], P('patch'), may hold values from -0.5 to 0.5
- retarded: float32 [2, 16, 56, 128, 128], P('lag', 'patch'), may hold values from -0.1875 to 0.1875
- block_rows: int32 [2, 16, 56], P('lag', 'patch'), may hold values from -1 to 3, as said below
- block_sources: int32 [2, 16, 56], P('lag', 'patch'), may hold values from -1 to 63, as said below
- owner_map: int32 [64], replicated, may hold values from 0 to 63, as said below
Outputs:
- currents: bfloat16 [4, 8192, 128], P(None, 'patch')
- fields_ahead: float32 [2, 8192, 128], P('lag', 'patch')
Inputs may be any that keep to these rules, and one draw needn't show every extreme that they name: `block_sources`: each device's list holds its live entries first and -1 after them; at most 56 live entries, a count that some device reaches in every draw; the live entries of one device name no (row, source) pair twice and, among them, at most one storage block of each patch owner. `block_rows`: -1 exactly where block_sources is -1. `owner_map`: A permutation of the 64 storage blocks; storage block q is owned by patch q // 4.
All inputs are finite; a program needn't handle non-finite values.
Results may differ from a plain program's by a relative error of at most 0.0055.
Values may be sent and summed in bfloat16 or wider, within the bound.
No kernel may reach another device: no remote copies, remote signals or barrier semaphores. Data moves between devices by JAX's collectives and lax.ppermute only.
A program may use at most 64 MiB of HBM per device.

v0:
```python
import jax
import jax.numpy as jnp
from jax import lax
from jax.experimental import pallas as pl
from jax.experimental.pallas import tpu as pltpu
from jax.sharding import PartitionSpec as P

VMEM = pl.BlockSpec(memory_space=pltpu.VMEM)
SMEM = pl.BlockSpec(memory_space=pltpu.SMEM)
HBM = pl.BlockSpec(memory_space=pltpu.HBM)
ANY = pl.BlockSpec(memory_space=pl.ANY)
DMA = pltpu.SemaphoreType.DMA
MIB = 1 << 20


def call(kernel, outs, in_specs, out_specs, scratch=(), flops=0, nbytes=MIB, aliases=None):
    return pl.pallas_call(
        kernel,
        out_shape=outs,
        in_specs=in_specs,
        out_specs=out_specs,
        scratch_shapes=scratch,
        input_output_aliases=aliases or {},
        cost_estimate=pl.CostEstimate(flops=flops, bytes_accessed=nbytes, transcendentals=0),
        compiler_params=pltpu.CompilerParams(vmem_limit_bytes=32 * MIB),
    )


def shape(dims, dtype):
    return jax.ShapeDtypeStruct(dims, dtype)


def started(*copies):
    copies = [pltpu.make_async_copy(*copy) for copy in copies]
    for copy in copies:
        copy.start()
    return copies


def request_kernel(per_patch, sources_hbm, owner_hbm, wanted, sources, owner_map, sems):
    copies = started(
        (sources_hbm, sources, sems.at[0]),
        (owner_hbm, owner_map, sems.at[1]),
    )
    patch = lax.broadcasted_iota(jnp.int32, wanted.shape, 0)
    for copy in copies:
        copy.wait()

    def entry(j, table):
        source = sources[0, 0, j]
        storage = owner_map[jnp.maximum(source, 0)]
        here = (patch == storage // per_patch) & (source >= 0)
        return jnp.where(here, storage % per_patch, table)

    wanted[...] = lax.fori_loop(
        0, sources.shape[2], entry, jnp.full(wanted.shape, -1, jnp.int32), unroll=8
    )


def panel_kernel(per_patch, rows, sources, owner_map, retarded, panel):
    size = retarded.shape[-1]
    panel[...] = jnp.zeros_like(panel)

    def entry(j, carry):
        source = sources[0, 0, j]

        @pl.when(source >= 0)
        def _():
            owner = owner_map[source] // per_patch
            row = pl.multiple_of(rows[0, 0, j] * size, size)
            column = pl.multiple_of(owner * size, size)
            block = retarded[0, 0, j]
            high = block.astype(panel.dtype)
            low = (block - high.astype(jnp.float32)).astype(panel.dtype)
            panel[0, pl.ds(row, size), pl.ds(column, size)] = high
            panel[1, pl.ds(row, size), pl.ds(column, size)] = low

        return carry

    lax.fori_loop(0, sources.shape[2], entry, 0)


def solved(excess, self_inverse):
    blocks, size, _ = self_inverse.shape
    parts = [
        jnp.dot(
            self_inverse[k],
            excess[k * size : (k + 1) * size],
            precision=lax.Precision.HIGHEST,
            preferred_element_type=jnp.float32,
        )
        for k in range(blocks)
    ]
    return jnp.concatenate(parts, axis=0).astype(jnp.bfloat16)


def product(panel, arrived):
    patches, size, columns = arrived.shape
    flat = arrived[...].reshape(patches * size, columns)
    high = jnp.dot(panel[0], flat, preferred_element_type=jnp.float32)
    return high + jnp.dot(panel[1], flat, preferred_element_type=jnp.float32)


def first_kernel(keeps, incident_hbm, own, received, inverse_hbm, current, incident, field, inverse, sems):
    copies = started(
        (incident_hbm.at[0], incident, sems.at[0]),
        (inverse_hbm, inverse, sems.at[1]),
    )
    mine = lax.axis_index("lag") < keeps

    @pl.when(mine)
    def _():
        started((own, field, sems.at[2]))[0].wait()

    @pl.when(jnp.logical_not(mine))
    def _():
        started((received, field, sems.at[2]))[0].wait()

    for copy in copies:
        copy.wait()
    current[...] = solved(incident[...].astype(jnp.float32) - field[...], inverse)


def solve_kernel(
    step, panel, arrived, field_hbm, incident_hbm, inverse_hbm, current, field, incident, inverse, sems
):
    @pl.when(lax.axis_index("lag") == 0)
    def _():
        copies = started(
            (field_hbm, field, sems.at[0]),
            (incident_hbm.at[step], incident, sems.at[1]),
            (inverse_hbm, inverse, sems.at[2]),
        )
        fresh = product(panel, arrived)
        for copy in copies:
            copy.wait()
        excess = incident[...].astype(jnp.float32) - (field[...] + fresh)
        current[...] = solved(excess, inverse)


def partial_kernel(panel, arrived, field_hbm, after, partial_hbm, field, sem):
    del after

    @pl.when(lax.axis_index("lag") > 0)
    def _():
        (copy,) = started((field_hbm, field, sem))
        fresh = product(panel, arrived)
        copy.wait()
        field[...] = field[...] + fresh
        started((field, partial_hbm, sem))[0].wait()


def ahead_kernel(panel, arrived, field_hbm, ahead, field, sem):
    (copy,) = started((field_hbm, field, sem))
    fresh = product(panel, arrived)
    copy.wait()
    ahead[...] = field[...] + fresh


def pack_kernel(step, keeps, asked, own, received, *refs):
    outgoing, currents, sems = refs[-3:]
    patches, size, _ = outgoing.shape

    def send(current):
        copies = [(current, currents.at[step], sems.at[patches])]
        for q in range(patches):
            start = pl.multiple_of(jnp.maximum(asked[q, 0, 0], 0) * size, size)
            copies.append((current.at[pl.ds(start, size)], outgoing.at[q], sems.at[q]))
        for copy in started(*copies):
            copy.wait()

    mine = lax.axis_index("lag") < keeps
    pl.when(mine)(lambda: send(own))
    pl.when(jnp.logical_not(mine))(lambda: send(received))


def shifted(x):
    sections = lax.axis_size("lag")
    return lax.ppermute(x, "lag", [(i, i - 1) for i in range(1, sections)])


def spread(x):
    sections = lax.axis_size("lag")
    section = lax.axis_index("lag")
    received, keeps = x, 1
    while keeps < sections:
        if keeps > 1:
            x = jnp.where(section < keeps // 2, x, received)
        pairs = [(i, i + keeps) for i in range(keeps) if i + keeps < sections]
        received = lax.ppermute(x, "lag", pairs)
        keeps *= 2
    return x, received, max(keeps // 2, 1)


def body(incident, pending, self_inverse, retarded, block_rows, block_sources, owner_map):
    steps, unknowns, columns = incident.shape
    per_patch, size, _ = self_inverse.shape
    listed = retarded.shape[2]
    patches = lax.axis_size("patch")
    bf16, f32 = jnp.bfloat16, jnp.float32
    all_flops = 4 * unknowns * patches * size * columns
    solve_flops = 12 * unknowns * size * columns
    panel_bytes = 4 * unknowns * patches * size
    column = (unknowns, columns)

    def exchange(x):
        return lax.all_to_all(x, "patch", split_axis=0, concat_axis=0, tiled=True)

    wanted = call(
        lambda *refs: request_kernel(per_patch, *refs),
        shape((patches, 1, 128), jnp.int32),
        [HBM, HBM],
        VMEM,
        [
            pltpu.SMEM(block_sources.shape, jnp.int32),
            pltpu.SMEM(owner_map.shape, jnp.int32),
            DMA((2,)),
        ],
    )(block_sources, owner_map)
    asked = exchange(wanted)
    own, received, keeps = spread(pending[0])
    current = call(
        lambda *refs: first_kernel(keeps, *refs),
        shape(column, bf16),
        [HBM] * 4,
        VMEM,
        [
            pltpu.VMEM(column, bf16),
            pltpu.VMEM(column, f32),
            pltpu.VMEM(self_inverse.shape, f32),
            DMA((3,)),
        ],
        solve_flops,
    )(incident, own, received, self_inverse)
    panel = call(
        lambda *refs: panel_kernel(per_patch, *refs),
        shape((2, unknowns, patches * size), bf16),
        [SMEM, SMEM, SMEM, VMEM],
        VMEM,
        nbytes=listed * size * size * 4 + panel_bytes,
    )(block_rows, block_sources, owner_map, retarded)

    own, received = current, current
    field = pending[0]
    currents = []
    for step in range(steps):
        outgoing, *currents = call(
            lambda *refs, n=step: pack_kernel(n, keeps, *refs),
            (shape((patches, size, columns), bf16), shape(incident.shape, bf16)),
            [SMEM, VMEM, VMEM] + [HBM] * len(currents),
            (HBM, HBM),
            [DMA((patches + 1,))],
            nbytes=4 * patches * size * columns,
            aliases={3: 1} if currents else None,
        )(asked, own, received, *currents)
        arrived = exchange(outgoing)
        field = shifted(field)
        if step + 1 < steps:
            current = call(
                lambda *refs, n=step + 1: solve_kernel(n, *refs),
                shape(column, bf16),
                [VMEM, VMEM, HBM, HBM, HBM],
                VMEM,
                [
                    pltpu.VMEM(column, f32),
                    pltpu.VMEM(column, bf16),
                    pltpu.VMEM(self_inverse.shape, f32),
                    DMA((3,)),
                ],
                all_flops + solve_flops,
                panel_bytes,
            )(panel, arrived, field, incident, self_inverse)
            own, received, keeps = spread(current)
            field = call(
                partial_kernel,
                shape(column, f32),
                [VMEM, VMEM, HBM, ANY],
                HBM,
                [pltpu.VMEM(column, f32), DMA],
                all_flops,
                panel_bytes,
            )(panel, arrived, field, current)
        else:
            field = call(
                ahead_kernel,
                shape(column, f32),
                [VMEM, VMEM, HBM],
                VMEM,
                [pltpu.VMEM(column, f32), DMA],
                all_flops,
                panel_bytes,
            )(panel, arrived, field)
    return currents[0], field[None]


def solution(mesh):
    in_specs = (
        P(None, "patch", None),
        P("lag", "patch", None),
        P("patch", None, None),
        P("lag", "patch", None, None, None),
        P("lag", "patch", None),
        P("lag", "patch", None),
        P(),
    )
    out_specs = (P(None, "patch", None), P("lag", "patch", None))
    return jax.shard_map(body, mesh=mesh, in_specs=in_specs, out_specs=out_specs, check_vma=False)
```

profile of v0, /device:TPU:0, one launch (start us, length us, event | category | flops | bytes accessed | tf_op | source)
XLA Modules:
  0.0 133.8 jit_solution(2216913853340162649)
XLA Ops:
  0.6 4.9 %collective-permute-start = (f32[512,128]{1,0:T(8,128)}, f32[512,128]{1,0:T(8,128)S(1)}, u32[]{:S(2)}, u32[]{:S(2)}) collective-permute-start(f32[512,128]{1,0:T(8,128)} %bitcast.2), channel_id=1, source_target_pairs={{0,16},{1,17},{2,18},{3,19},{4,20},{5,21},{6,22},{7,23},{8,24},{9,... | collective-permute-start | bytes 786440 | tf_op jit(solution)/shard_map/ppermute | solution.py:190
  6.8 1.7 %shard_map.86 = s32[16,1,128]{2,1,0:T(1,128)} custom-call(s32[1,1,56]{2,1,0:T(1,128)S(1)} %copy-done.14, s32[64]{0:T(128)S(1)} %copy-done.16), custom_call_target="tpu_custom_call" | custom-call | bytes 1048576 | tf_op jit(solution)/shard_map/pallas_call | solution.py:209
  8.5 5.9 %all-to-all-start = ((s32[16,1,128]{2,1,0:T(1,128)}), s32[16,1,128]{2,1,0:T(1,128)S(1)}, u32[]{:S(2)}, u32[]{:S(2)}) async-start(s32[16,1,128]{2,1,0:T(1,128)} %shard_map.86), calls=%async_computation | async-start | bytes 16384 | tf_op jit(solution)/shard_map/all_to_all | solution.py:207
  18.0 2.8 %all-to-all-done.refs_0_ = s32[16,1,128]{2,1,0:T(1,128)S(1)} async-done(((s32[16,1,128]{2,1,0:T(1,128)}), s32[16,1,128]{2,1,0:T(1,128)S(1)}, u32[]{:S(2)}, u32[]{:S(2)}) %all-to-all-start) | async-done | bytes 8224 | tf_op jit(solution)/shard_map/all_to_all | solution.py:207
  20.8 1.6 %shard_map.89 = (bf16[16,128,128]{2,1,0:T(8,128)(2,1)}, bf16[4,512,128]{2,1,0:T(8,128)(2,1)}) custom-call(s32[16,1,128]{2,1,0:T(1,128)S(1)} %all-to-all-done.refs_0_, bf16[512,128]{1,0:T(8,128)(2,1)S(1)} %shard_map.88.refs_1_.refs_2_, bf16[512,128]{1,0:T(8,128)(2,1)S(1)} %shard_map.88.refs_1_.refs_2_), custom_call_target="tpu_custom_call" | custom-call | bytes 1048576 | tf_op jit(solution)/shard_map/pallas_call | solution.py:247
  22.4 3.6 %all-to-all-start.1 = ((bf16[16,128,128]{2,1,0:T(8,128)(2,1)}), bf16[16,128,128]{2,1,0:T(8,128)(2,1)S(1)}, u32[]{:S(2)}, u32[]{:S(2)}) async-start(bf16[16,128,128]{2,1,0:T(8,128)(2,1)} %get-tuple-element.10), calls=%async_computation.1 | async-start | bytes 1048576 | tf_op jit(solution)/shard_map/all_to_all | solution.py:207
  27.5 2.0 %copy-done.12 = f32[1,1,56,128,128]{4,3,2,1,0:T(8,128)S(1)} copy-done((f32[1,1,56,128,128]{4,3,2,1,0:T(8,128)S(1)}, f32[1,1,56,128,128]{4,3,2,1,0:T(8,128)}, u32[]{:S(2)}) %copy-start.12) | copy-done | bytes 3670040
  31.5 2.4 %shard_map.87.refs_0_.panel = bf16[2,512,2048]{2,1,0:T(8,128)(2,1)S(1)} custom-call(s32[1,1,56]{2,1,0:T(1,128)S(1)} %copy-done.18, s32[1,1,56]{2,1,0:T(1,128)S(1)} %copy-done.15, s32[64]{0:T(128)S(1)} %copy-done.17, f32[1,1,56,128,128]{4,3,2,1,0:T(8,128)S(1)} %copy-done.12), custom_call_target="tpu_custom_call" | custom-call | bytes 7864320 | tf_op jit(solution)/shard_map/pallas_call | solution.py:235
  33.9 2.0 %copy-done = bf16[2,512,2048]{2,1,0:T(8,128)(2,1)} copy-done((bf16[2,512,2048]{2,1,0:T(8,128)(2,1)}, bf16[2,512,2048]{2,1,0:T(8,128)(2,1)S(1)}, u32[]{:S(2)}) %copy-start) | copy-done | bytes 4194328
  36.8 3.7 %all-to-all-done.1.refs_1_.arrived = bf16[16,128,128]{2,1,0:T(8,128)(2,1)S(1)} async-done(((bf16[16,128,128]{2,1,0:T(8,128)(2,1)}), bf16[16,128,128]{2,1,0:T(8,128)(2,1)S(1)}, u32[]{:S(2)}, u32[]{:S(2)}) %all-to-all-start.1) | async-done | bytes 524320 | tf_op jit(solution)/shard_map/all_to_all | solution.py:207
  40.4 2.2 %copy-done.1 = bf16[2,512,2048]{2,1,0:T(8,128)(2,1)S(1)} copy-done((bf16[2,512,2048]{2,1,0:T(8,128)(2,1)S(1)}, bf16[2,512,2048]{2,1,0:T(8,128)(2,1)}, u32[]{:S(2)}) %copy-start.1) | copy-done | bytes 4194328
  42.6 1.9 %shard_map.90.refs_1_.after = bf16[512,128]{1,0:T(8,128)(2,1)S(1)} custom-call(bf16[2,512,2048]{2,1,0:T(8,128)(2,1)S(1)} %copy-done.1, bf16[16,128,128]{2,1,0:T(8,128)(2,1)S(1)} %all-to-all-done.1.refs_1_.arrived, f32[512,128]{1,0:T(8,128)S(1)} %collective-permute-done.1.refs_2_.field_hbm, bf16[4,512,128]{2,1,0:T(8,128)(2,1)S(1)} %copy-done.9, ...), custom_call_target="tpu_custom_call" | custom-call | flops 637534208 | bytes 4194304 | tf_op jit(solution)/shard_map/pallas_call | solution.py:259
  45.8 3.2 %collective-permute-done.2.refs_2_ = bf16[512,128]{1,0:T(8,128)(2,1)S(1)} collective-permute-done((bf16[512,128]{1,0:T(8,128)(2,1)S(1)}, bf16[512,128]{1,0:T(8,128)(2,1)S(1)}, u32[]{:S(2)}, u32[]{:S(2)}) %collective-permute-start.2) | collective-permute-done | bytes 131104 | tf_op jit(solution)/shard_map/ppermute | solution.py:190
  50.7 4.3 %all-to-all-start.2 = ((bf16[16,128,128]{2,1,0:T(8,128)(2,1)}), bf16[16,128,128]{2,1,0:T(8,128)(2,1)S(1)}, u32[]{:S(2)}, u32[]{:S(2)}) async-start(bf16[16,128,128]{2,1,0:T(8,128)(2,1)} %get-tuple-element.12), calls=%async_computation.2 | async-start | bytes 1048576 | tf_op jit(solution)/shard_map/all_to_all | solution.py:207
  55.0 2.2 %copy-done.2 = bf16[2,512,2048]{2,1,0:T(8,128)(2,1)S(1)} copy-done((bf16[2,512,2048]{2,1,0:T(8,128)(2,1)S(1)}, bf16[2,512,2048]{2,1,0:T(8,128)(2,1)}, u32[]{:S(2)}) %copy-start.2) | copy-done | bytes 4194328
  58.5 10.7 %collective-permute-done.3.refs_2_.field_hbm = f32[512,128]{1,0:T(8,128)S(1)} collective-permute-done((f32[512,128]{1,0:T(8,128)S(1)}, f32[512,128]{1,0:T(8,128)S(1)}, u32[]{:S(2)}, u32[]{:S(2)}) %collective-permute-start.3) | collective-permute-done | bytes 262176 | tf_op jit(solution)/shard_map/ppermute | solution.py:179
  69.5 2.2 %copy-done.3 = bf16[2,512,2048]{2,1,0:T(8,128)(2,1)S(1)} copy-done((bf16[2,512,2048]{2,1,0:T(8,128)(2,1)S(1)}, bf16[2,512,2048]{2,1,0:T(8,128)(2,1)}, u32[]{:S(2)}) %copy-start.3) | copy-done | bytes 4194328
  71.6 1.9 %shard_map.93.refs_1_.after = bf16[512,128]{1,0:T(8,128)(2,1)S(1)} custom-call(bf16[2,512,2048]{2,1,0:T(8,128)(2,1)S(1)} %copy-done.3, bf16[16,128,128]{2,1,0:T(8,128)(2,1)S(1)} %all-to-all-done.2.refs_1_.arrived, f32[512,128]{1,0:T(8,128)S(1)} %collective-permute-done.3.refs_2_.field_hbm, bf16[4,512,128]{2,1,0:T(8,128)(2,1)S(1)} %copy-done.9, ...), custom_call_target="tpu_custom_call" | custom-call | flops 637534208 | bytes 4194304 | tf_op jit(solution)/shard_map/pallas_call | solution.py:259
  73.5 2.5 %collective-permute-start.4 = (bf16[512,128]{1,0:T(8,128)(2,1)S(1)}, bf16[512,128]{1,0:T(8,128)(2,1)S(1)}, u32[]{:S(2)}, u32[]{:S(2)}) collective-permute-start(bf16[512,128]{1,0:T(8,128)(2,1)S(1)} %shard_map.93.refs_1_.after), channel_id=1, source_target_pairs={{0,16},{1,17},{2,18},{3,19},{4,20},{5,21},{6,22},{7,23},{8,24},{9,... | collective-permute-start | bytes 393224 | tf_op jit(solution)/shard_map/ppermute | solution.py:190
  76.1 2.9 %collective-permute-done.4.refs_2_ = bf16[512,128]{1,0:T(8,128)(2,1)S(1)} collective-permute-done((bf16[512,128]{1,0:T(8,128)(2,1)S(1)}, bf16[512,128]{1,0:T(8,128)(2,1)S(1)}, u32[]{:S(2)}, u32[]{:S(2)}) %collective-permute-start.4) | collective-permute-done | bytes 131104 | tf_op jit(solution)/shard_map/ppermute | solution.py:190
  80.6 4.4 %all-to-all-start.3 = ((bf16[16,128,128]{2,1,0:T(8,128)(2,1)}), bf16[16,128,128]{2,1,0:T(8,128)(2,1)S(1)}, u32[]{:S(2)}, u32[]{:S(2)}) async-start(bf16[16,128,128]{2,1,0:T(8,128)(2,1)} %get-tuple-element.14), calls=%async_computation.3 | async-start | bytes 1048576 | tf_op jit(solution)/shard_map/all_to_all | solution.py:207
  85.1 2.2 %copy-done.4 = bf16[2,512,2048]{2,1,0:T(8,128)(2,1)S(1)} copy-done((bf16[2,512,2048]{2,1,0:T(8,128)(2,1)S(1)}, bf16[2,512,2048]{2,1,0:T(8,128)(2,1)}, u32[]{:S(2)}) %copy-start.4) | copy-done | bytes 4194328
  88.5 10.7 %collective-permute-done.5.refs_2_.field_hbm = f32[512,128]{1,0:T(8,128)S(1)} collective-permute-done((f32[512,128]{1,0:T(8,128)S(1)}, f32[512,128]{1,0:T(8,128)S(1)}, u32[]{:S(2)}, u32[]{:S(2)}) %collective-permute-start.5) | collective-permute-done | bytes 262176 | tf_op jit(solution)/shard_map/ppermute | solution.py:179
  99.5 2.2 %copy-done.5 = bf16[2,512,2048]{2,1,0:T(8,128)(2,1)S(1)} copy-done((bf16[2,512,2048]{2,1,0:T(8,128)(2,1)S(1)}, bf16[2,512,2048]{2,1,0:T(8,128)(2,1)}, u32[]{:S(2)}) %copy-start.5) | copy-done | bytes 4194328
  101.7 1.9 %shard_map.96.refs_1_.after = bf16[512,128]{1,0:T(8,128)(2,1)S(1)} custom-call(bf16[2,512,2048]{2,1,0:T(8,128)(2,1)S(1)} %copy-done.5, bf16[16,128,128]{2,1,0:T(8,128)(2,1)S(1)} %all-to-all-done.3.refs_1_.arrived, f32[512,128]{1,0:T(8,128)S(1)} %collective-permute-done.5.refs_2_.field_hbm, bf16[4,512,128]{2,1,0:T(8,128)(2,1)S(1)} %copy-done.9, ...), custom_call_target="tpu_custom_call" | custom-call | flops 637534208 | bytes 4194304 | tf_op jit(solution)/shard_map/pallas_call | solution.py:259
  103.6 2.5 %collective-permute-start.6 = (bf16[512,128]{1,0:T(8,128)(2,1)S(1)}, bf16[512,128]{1,0:T(8,128)(2,1)S(1)}, u32[]{:S(2)}, u32[]{:S(2)}) collective-permute-start(bf16[512,128]{1,0:T(8,128)(2,1)S(1)} %shard_map.96.refs_1_.after), channel_id=1, source_target_pairs={{0,16},{1,17},{2,18},{3,19},{4,20},{5,21},{6,22},{7,23},{8,24},{9,... | collective-permute-start | bytes 393224 | tf_op jit(solution)/shard_map/ppermute | solution.py:190
  106.1 2.9 %collective-permute-done.6.refs_2_ = bf16[512,128]{1,0:T(8,128)(2,1)S(1)} collective-permute-done((bf16[512,128]{1,0:T(8,128)(2,1)S(1)}, bf16[512,128]{1,0:T(8,128)(2,1)S(1)}, u32[]{:S(2)}, u32[]{:S(2)}) %collective-permute-start.6) | collective-permute-done | bytes 131104 | tf_op jit(solution)/shard_map/ppermute | solution.py:190
  110.7 4.4 %all-to-all-start.4 = ((bf16[16,128,128]{2,1,0:T(8,128)(2,1)}), bf16[16,128,128]{2,1,0:T(8,128)(2,1)S(1)}, u32[]{:S(2)}, u32[]{:S(2)}) async-start(bf16[16,128,128]{2,1,0:T(8,128)(2,1)} %get-tuple-element.17), calls=%async_computation.4 | async-start | bytes 1048576 | tf_op jit(solution)/shard_map/all_to_all | solution.py:207
  115.1 2.2 %copy-done.6 = bf16[2,512,2048]{2,1,0:T(8,128)(2,1)S(1)} copy-done((bf16[2,512,2048]{2,1,0:T(8,128)(2,1)S(1)}, bf16[2,512,2048]{2,1,0:T(8,128)(2,1)}, u32[]{:S(2)}) %copy-start.6) | copy-done | bytes 4194328
  118.6 10.7 %collective-permute-done.7.field_hbm = f32[512,128]{1,0:T(8,128)S(1)} collective-permute-done((f32[512,128]{1,0:T(8,128)S(1)}, f32[512,128]{1,0:T(8,128)S(1)}, u32[]{:S(2)}, u32[]{:S(2)}) %collective-permute-start.7) | collective-permute-done | bytes 262176 | tf_op jit(solution)/shard_map/ppermute | solution.py:179
  129.6 2.2 %copy-done.7 = bf16[2,512,2048]{2,1,0:T(8,128)(2,1)S(1)} copy-done((bf16[2,512,2048]{2,1,0:T(8,128)(2,1)S(1)}, bf16[2,512,2048]{2,1,0:T(8,128)(2,1)}, u32[]{:S(2)}) %copy-start.7) | copy-done | bytes 4194328
  131.8 2.0 %shard_map.99 = f32[512,128]{1,0:T(8,128)} custom-call(bf16[2,512,2048]{2,1,0:T(8,128)(2,1)S(1)} %copy-done.7, bf16[16,128,128]{2,1,0:T(8,128)(2,1)S(1)} %all-to-all-done.4.arrived, f32[512,128]{1,0:T(8,128)S(1)} %collective-permute-done.7.field_hbm), custom_call_target="tpu_custom_call" | custom-call | flops 536870912 | bytes 4194304 | tf_op jit(solution)/shard_map/pallas_call | solution.py:284
  (46 shorter events, 20.2 us)
Async XLA Ops:
  0.6 13.8 %collective-permute-start = (f32[512,128]{1,0:T(8,128)}, f32[512,128]{1,0:T(8,128)S(1)}, u32[]{:S(2)}, u32[]{:S(2)}) collective-permute-start(f32[512,128]{1,0:T(8,128)} %bitcast.2), channel_id=1, source_target_pairs={{0,16},{1,17},{2,18},{3,19},{4,20},{5,21},{6,22},{7,23},{8,24},{9,... | collective-permute-start | bytes 786440 | tf_op jit(solution)/shard_map/ppermute | solution.py:190
  5.5 0.7 copy-start.14
  6.2 0.7 copy-start.16
  8.5 12.3 %all-to-all-start = ((s32[16,1,128]{2,1,0:T(1,128)}), s32[16,1,128]{2,1,0:T(1,128)S(1)}, u32[]{:S(2)}, u32[]{:S(2)}) async-start(s32[16,1,128]{2,1,0:T(1,128)} %shard_map.86), calls=%async_computation | async-start | bytes 16384 | tf_op jit(solution)/shard_map/all_to_all | solution.py:207
  14.5 1.0 copy-start.8
  15.5 0.9 copy-start.10
  16.4 0.9 copy-start.13
  22.4 18.0 %all-to-all-start.1 = ((bf16[16,128,128]{2,1,0:T(8,128)(2,1)}), bf16[16,128,128]{2,1,0:T(8,128)(2,1)S(1)}, u32[]{:S(2)}, u32[]{:S(2)}) async-start(bf16[16,128,128]{2,1,0:T(8,128)(2,1)} %get-tuple-element.10), calls=%async_computation.1 | async-start | bytes 1048576 | tf_op jit(solution)/shard_map/all_to_all | solution.py:207
  26.0 14.4 %copy-start.9 = (bf16[4,512,128]{2,1,0:T(8,128)(2,1)S(1)}, bf16[4,512,128]{2,1,0:T(8,128)(2,1)}, u32[]{:S(2)}) copy-start(bf16[4,512,128]{2,1,0:T(8,128)(2,1)} %refs_3_.9) | copy-start | bytes 1572868
  26.0 14.4 %copy-start.11 = (f32[4,128,128]{2,1,0:T(8,128)S(1)}, f32[4,128,128]{2,1,0:T(8,128)}, u32[]{:S(2)}) copy-start(f32[4,128,128]{2,1,0:T(8,128)} %refs_4_.5) | copy-start | bytes 786436
  26.0 10.7 %collective-permute-start.1 = (f32[512,128]{1,0:T(8,128)}, f32[512,128]{1,0:T(8,128)S(1)}, u32[]{:S(2)}, u32[]{:S(2)}) collective-permute-start(f32[512,128]{1,0:T(8,128)} %bitcast.3), channel_id=1, source_target_pairs={{16,0},{17,1},{18,2},{19,3},{20,4},{21,5},{22,6},{23,7},{24,8},{25... | collective-permute-start | bytes 786440 | tf_op jit(solution)/shard_map/ppermute | solution.py:179
  27.5 2.0 %copy-start.12 = (f32[1,1,56,128,128]{4,3,2,1,0:T(8,128)S(1)}, f32[1,1,56,128,128]{4,3,2,1,0:T(8,128)}, u32[]{:S(2)}) copy-start(f32[1,1,56,128,128]{4,3,2,1,0:T(8,128)} %refs_3_.5) | copy-start | bytes 11010052
  29.5 0.7 copy-start.15
  30.2 0.7 copy-start.17
  30.8 0.7 copy-start.18
  33.9 2.0 %copy-start = (bf16[2,512,2048]{2,1,0:T(8,128)(2,1)}, bf16[2,512,2048]{2,1,0:T(8,128)(2,1)S(1)}, u32[]{:S(2)}) copy-start(bf16[2,512,2048]{2,1,0:T(8,128)(2,1)S(1)} %shard_map.87.refs_0_.panel) | copy-start | bytes 12582916
  40.4 2.2 %copy-start.1 = (bf16[2,512,2048]{2,1,0:T(8,128)(2,1)S(1)}, bf16[2,512,2048]{2,1,0:T(8,128)(2,1)}, u32[]{:S(2)}) copy-start(bf16[2,512,2048]{2,1,0:T(8,128)(2,1)} %copy-done) | copy-start | bytes 12582916
  44.5 4.5 %collective-permute-start.2 = (bf16[512,128]{1,0:T(8,128)(2,1)S(1)}, bf16[512,128]{1,0:T(8,128)(2,1)S(1)}, u32[]{:S(2)}, u32[]{:S(2)}) collective-permute-start(bf16[512,128]{1,0:T(8,128)(2,1)S(1)} %shard_map.90.refs_1_.after), channel_id=1, source_target_pairs={{0,16},{1,17},{2,18},{3,19},{4,20},{5,21},{6,22},{7,23},{8,24},{9,... | collective-permute-start | bytes 393224 | tf_op jit(solution)/shard_map/ppermute | solution.py:190
  50.7 18.8 %all-to-all-start.2 = ((bf16[16,128,128]{2,1,0:T(8,128)(2,1)}), bf16[16,128,128]{2,1,0:T(8,128)(2,1)S(1)}, u32[]{:S(2)}, u32[]{:S(2)}) async-start(bf16[16,128,128]{2,1,0:T(8,128)(2,1)} %get-tuple-element.12), calls=%async_computation.2 | async-start | bytes 1048576 | tf_op jit(solution)/shard_map/all_to_all | solution.py:207
  55.0 2.2 %copy-start.2 = (bf16[2,512,2048]{2,1,0:T(8,128)(2,1)S(1)}, bf16[2,512,2048]{2,1,0:T(8,128)(2,1)}, u32[]{:S(2)}) copy-start(bf16[2,512,2048]{2,1,0:T(8,128)(2,1)} %copy-done) | copy-start | bytes 12582916
  57.2 12.0 %collective-permute-start.3 = (f32[512,128]{1,0:T(8,128)S(1)}, f32[512,128]{1,0:T(8,128)S(1)}, u32[]{:S(2)}, u32[]{:S(2)}) collective-permute-start(f32[512,128]{1,0:T(8,128)S(1)} %shard_map.92), channel_id=1, source_target_pairs={{16,0},{17,1},{18,2},{19,3},{20,4},{21,5},{22,6},{23,7},{24,8},{25... | collective-permute-start | bytes 786440 | tf_op jit(solution)/shard_map/ppermute | solution.py:179
  69.5 2.2 %copy-start.3 = (bf16[2,512,2048]{2,1,0:T(8,128)(2,1)S(1)}, bf16[2,512,2048]{2,1,0:T(8,128)(2,1)}, u32[]{:S(2)}) copy-start(bf16[2,512,2048]{2,1,0:T(8,128)(2,1)} %copy-done) | copy-start | bytes 12582916
  73.5 5.5 %collective-permute-start.4 = (bf16[512,128]{1,0:T(8,128)(2,1)S(1)}, bf16[512,128]{1,0:T(8,128)(2,1)S(1)}, u32[]{:S(2)}, u32[]{:S(2)}) collective-permute-start(bf16[512,128]{1,0:T(8,128)(2,1)S(1)} %shard_map.93.refs_1_.after), channel_id=1, source_target_pairs={{0,16},{1,17},{2,18},{3,19},{4,20},{5,21},{6,22},{7,23},{8,24},{9,... | collective-permute-start | bytes 393224 | tf_op jit(solution)/shard_map/ppermute | solution.py:190
  80.6 18.9 %all-to-all-start.3 = ((bf16[16,128,128]{2,1,0:T(8,128)(2,1)}), bf16[16,128,128]{2,1,0:T(8,128)(2,1)S(1)}, u32[]{:S(2)}, u32[]{:S(2)}) async-start(bf16[16,128,128]{2,1,0:T(8,128)(2,1)} %get-tuple-element.14), calls=%async_computation.3 | async-start | bytes 1048576 | tf_op jit(solution)/shard_map/all_to_all | solution.py:207
  85.0 2.2 %copy-start.4 = (bf16[2,512,2048]{2,1,0:T(8,128)(2,1)S(1)}, bf16[2,512,2048]{2,1,0:T(8,128)(2,1)}, u32[]{:S(2)}) copy-start(bf16[2,512,2048]{2,1,0:T(8,128)(2,1)} %copy-done) | copy-start | bytes 12582916
  87.2 12.0 %collective-permute-start.5 = (f32[512,128]{1,0:T(8,128)S(1)}, f32[512,128]{1,0:T(8,128)S(1)}, u32[]{:S(2)}, u32[]{:S(2)}) collective-permute-start(f32[512,128]{1,0:T(8,128)S(1)} %shard_map.95), channel_id=1, source_target_pairs={{16,0},{17,1},{18,2},{19,3},{20,4},{21,5},{22,6},{23,7},{24,8},{25... | collective-permute-start | bytes 786440 | tf_op jit(solution)/shard_map/ppermute | solution.py:179
  99.5 2.2 %copy-start.5 = (bf16[2,512,2048]{2,1,0:T(8,128)(2,1)S(1)}, bf16[2,512,2048]{2,1,0:T(8,128)(2,1)}, u32[]{:S(2)}) copy-start(bf16[2,512,2048]{2,1,0:T(8,128)(2,1)} %copy-done) | copy-start | bytes 12582916
  103.6 5.5 %collective-permute-start.6 = (bf16[512,128]{1,0:T(8,128)(2,1)S(1)}, bf16[512,128]{1,0:T(8,128)(2,1)S(1)}, u32[]{:S(2)}, u32[]{:S(2)}) collective-permute-start(bf16[512,128]{1,0:T(8,128)(2,1)S(1)} %shard_map.96.refs_1_.after), channel_id=1, source_target_pairs={{0,16},{1,17},{2,18},{3,19},{4,20},{5,21},{6,22},{7,23},{8,24},{9,... | collective-permute-start | bytes 393224 | tf_op jit(solution)/shard_map/ppermute | solution.py:190
  110.7 18.9 %all-to-all-start.4 = ((bf16[16,128,128]{2,1,0:T(8,128)(2,1)}), bf16[16,128,128]{2,1,0:T(8,128)(2,1)S(1)}, u32[]{:S(2)}, u32[]{:S(2)}) async-start(bf16[16,128,128]{2,1,0:T(8,128)(2,1)} %get-tuple-element.17), calls=%async_computation.4 | async-start | bytes 1048576 | tf_op jit(solution)/shard_map/all_to_all | solution.py:207
  115.1 2.2 %copy-start.6 = (bf16[2,512,2048]{2,1,0:T(8,128)(2,1)S(1)}, bf16[2,512,2048]{2,1,0:T(8,128)(2,1)}, u32[]{:S(2)}) copy-start(bf16[2,512,2048]{2,1,0:T(8,128)(2,1)} %copy-done) | copy-start | bytes 12582916
  117.3 12.0 %collective-permute-start.7 = (f32[512,128]{1,0:T(8,128)S(1)}, f32[512,128]{1,0:T(8,128)S(1)}, u32[]{:S(2)}, u32[]{:S(2)}) collective-permute-start(f32[512,128]{1,0:T(8,128)S(1)} %shard_map.98), channel_id=1, source_target_pairs={{16,0},{17,1},{18,2},{19,3},{20,4},{21,5},{22,6},{23,7},{24,8},{25... | collective-permute-start | bytes 786440 | tf_op jit(solution)/shard_map/ppermute | solution.py:179
  129.6 2.2 %copy-start.7 = (bf16[2,512,2048]{2,1,0:T(8,128)(2,1)S(1)}, bf16[2,512,2048]{2,1,0:T(8,128)(2,1)}, u32[]{:S(2)}) copy-start(bf16[2,512,2048]{2,1,0:T(8,128)(2,1)} %copy-done) | copy-start | bytes 12582916
where the time goes:
time: 135 us; the launch traced here: 134 us
  waiting for transfers between devices  49.2 us (36%)
  starting transfers between devices  39.2 us (29%)
  local copies, waits for them, and re-layouts  25.5 us (19%)
  Pallas kernels  18.9 us (14%)
    ppermute x4, waiting for transfers between devices, shifted(): return lax.ppermute(x, 'lag', [(i, i - 1) for i in range(1, sections)])  32.9 us
    unnamed x38, local copies, waits for them, and re-layouts  25.5 us
    all_to_all x5, starting transfers between devices, exchange(): return lax.all_to_all(x, 'patch', split_axis=0, concat_axis=0, tiled=True)  22.6 us
    ppermute x4, starting transfers between devices, spread(): received = lax.ppermute(x, 'lag', pairs)  11.3 us
    ppermute x4, waiting for transfers between devices, spread(): received = lax.ppermute(x, 'lag', pairs)  9.02 us
    all_to_all x5, waiting for transfers between devices, exchange(): return lax.all_to_all(x, 'patch', split_axis=0, concat_axis=0, tiled=True)  7.34 us
    pallas_call x4, Pallas kernels, body(): call(lambda *refs, n=step: pack_kernel(n, keeps, *refs), (shape((patches,...  6.56 us
    pallas_call x3, Pallas kernels, body(): call(lambda *refs, n=step + 1: solve_kernel(n, *refs), shape(column, bf16...  5.64 us
  transfers between devices with their start and end apart: 13, of which 12 were waited for; matrix products, arithmetic and copies ran while one was open for 0% of the time, Pallas kernels for 4%

commit v1 on v0

--- a/solution.py
+++ b/solution.py
@@ -13,7 +13,7 @@
 MIB = 1 << 20
 
 
-def call(kernel, outs, in_specs, out_specs, scratch=(), flops=0, nbytes=MIB, aliases=None):
+def call(kernel, outs, in_specs, out_specs, scratch=(), flops=0, nbytes=0, vmem=0, aliases=None):
     return pl.pallas_call(
         kernel,
         out_shape=outs,
@@ -22,7 +22,7 @@
         scratch_shapes=scratch,
         input_output_aliases=aliases or {},
         cost_estimate=pl.CostEstimate(flops=flops, bytes_accessed=nbytes, transcendentals=0),
-        compiler_params=pltpu.CompilerParams(vmem_limit_bytes=32 * MIB),
+        compiler_params=pltpu.CompilerParams(vmem_limit_bytes=vmem + 6 * MIB),
     )
 
 
@@ -101,28 +101,23 @@
     return high + jnp.dot(panel[1], flat, preferred_element_type=jnp.float32)
 
 
-def first_kernel(keeps, incident_hbm, own, received, inverse_hbm, current, incident, field, inverse, sems):
-    copies = started(
-        (incident_hbm.at[0], incident, sems.at[0]),
-        (inverse_hbm, inverse, sems.at[1]),
-    )
-    mine = lax.axis_index("lag") < keeps
-
-    @pl.when(mine)
+def first_kernel(incident_hbm, field_hbm, inverse_hbm, after, current, incident, field, inverse, sems):
+    del after
+
+    @pl.when(lax.axis_index("lag") == 0)
     def _():
-        started((own, field, sems.at[2]))[0].wait()
-
-    @pl.when(jnp.logical_not(mine))
-    def _():
-        started((received, field, sems.at[2]))[0].wait()
-
-    for copy in copies:
-        copy.wait()
-    current[...] = solved(incident[...].astype(jnp.float32) - field[...], inverse)
+        copies = started(
+            (incident_hbm.at[0], incident, sems.at[0]),
+            (inverse_hbm, inverse, sems.at[1]),
+            (field_hbm, field, sems.at[2]),
+        )
+        for copy in copies:
+            copy.wait()
+        current[...] = solved(incident[...].astype(jnp.float32) - field[...], inverse)
 
 
 def solve_kernel(
-    step, panel, arrived, field_hbm, incident_hbm, inverse_hbm, current, field, incident, inverse, sems
+    step, panel, arrived, field_hbm, incident_hbm, inverse_hbm, current, incident, field, inverse, sems
 ):
     @pl.when(lax.axis_index("lag") == 0)
     def _():
@@ -157,21 +152,23 @@
     ahead[...] = field[...] + fresh
 
 
-def pack_kernel(step, keeps, asked, own, received, *refs):
-    outgoing, currents, sems = refs[-3:]
+def pack_kernel(step, keeps, early, asked_any, current, *refs):
+    outgoing, currents, asked, sems = refs[-4:]
     patches, size, _ = outgoing.shape
-
-    def send(current):
-        copies = [(current, currents.at[step], sems.at[patches])]
+    section = lax.axis_index("lag")
+
+    @pl.when(section < keeps if early else section >= keeps)
+    def _():
+        (copy,) = started((asked_any, asked, sems.at[0]))
+        (whole,) = started((current, currents.at[step], sems.at[patches]))
+        copy.wait()
+        copies = []
         for q in range(patches):
             start = pl.multiple_of(jnp.maximum(asked[q, 0, 0], 0) * size, size)
             copies.append((current.at[pl.ds(start, size)], outgoing.at[q], sems.at[q]))
         for copy in started(*copies):
             copy.wait()
-
-    mine = lax.axis_index("lag") < keeps
-    pl.when(mine)(lambda: send(own))
-    pl.when(jnp.logical_not(mine))(lambda: send(received))
+        whole.wait()
 
 
 def shifted(x):
@@ -203,8 +200,28 @@
     panel_bytes = 4 * unknowns * patches * size
     column = (unknowns, columns)
 
+    column_bytes = 4 * unknowns * columns
+    arrived_bytes = 2 * patches * size * columns
+
     def exchange(x):
         return lax.all_to_all(x, "patch", split_axis=0, concat_axis=0, tiled=True)
+
+    def pack(step, keeps, early, current, filled, after):
+        held = [x for x in filled if x is not None]
+        first_held = 2 + len(after)
+        aliases = {}
+        for out, x in enumerate(filled):
+            if x is not None:
+                aliases[first_held + len(aliases)] = out
+        return call(
+            lambda *refs: pack_kernel(step, keeps, early, *refs),
+            (shape((patches, size, columns), bf16), shape(incident.shape, bf16)),
+            [ANY, VMEM] + [ANY] * len(after) + [HBM] * len(held),
+            (HBM, HBM),
+            [pltpu.SMEM(asked.shape, jnp.int32), DMA((patches + 1,))],
+            vmem=column_bytes,
+            aliases=aliases,
+        )(asked, current, *after, *held)
 
     wanted = call(
         lambda *refs: request_kernel(per_patch, *refs),
@@ -218,41 +235,38 @@
         ],
     )(block_sources, owner_map)
     asked = exchange(wanted)
-    own, received, keeps = spread(pending[0])
+    solve_scratch = [
+        pltpu.VMEM(column, bf16),
+        pltpu.VMEM(column, f32),
+        pltpu.VMEM(self_inverse.shape, f32),
+        DMA((3,)),
+    ]
     current = call(
-        lambda *refs: first_kernel(keeps, *refs),
+        first_kernel,
         shape(column, bf16),
-        [HBM] * 4,
+        [HBM, HBM, HBM, ANY],
         VMEM,
-        [
-            pltpu.VMEM(column, bf16),
-            pltpu.VMEM(column, f32),
-            pltpu.VMEM(self_inverse.shape, f32),
-            DMA((3,)),
-        ],
+        solve_scratch,
         solve_flops,
-    )(incident, own, received, self_inverse)
+        vmem=4 * column_bytes,
+    )(incident, pending[0], self_inverse, wanted)
     panel = call(
         lambda *refs: panel_kernel(per_patch, *refs),
         shape((2, unknowns, patches * size), bf16),
         [SMEM, SMEM, SMEM, VMEM],
         VMEM,
         nbytes=listed * size * size * 4 + panel_bytes,
+        vmem=listed * size * size * 4 + panel_bytes,
     )(block_rows, block_sources, owner_map, retarded)
 
-    own, received = current, current
     field = pending[0]
-    currents = []
+    currents = None
+    after = []
     for step in range(steps):
-        outgoing, *currents = call(
-            lambda *refs, n=step: pack_kernel(n, keeps, *refs),
-            (shape((patches, size, columns), bf16), shape(incident.shape, bf16)),
-            [SMEM, VMEM, VMEM] + [HBM] * len(currents),
-            (HBM, HBM),
-            [DMA((patches + 1,))],
-            nbytes=4 * patches * size * columns,
-            aliases={3: 1} if currents else None,
-        )(asked, own, received, *currents)
+        own, received, keeps = spread(current)
+        outgoing, currents = pack(step, keeps, True, own, (None, currents), [])
+        if lax.axis_size("lag") > 1:
+            outgoing, currents = pack(step, keeps, False, received, (outgoing, currents), after)
         arrived = exchange(outgoing)
         field = shifted(field)
         if step + 1 < steps:
@@ -261,16 +275,11 @@
                 shape(column, bf16),
                 [VMEM, VMEM, HBM, HBM, HBM],
                 VMEM,
-                [
-                    pltpu.VMEM(column, f32),
-                    pltpu.VMEM(column, bf16),
-                    pltpu.VMEM(self_inverse.shape, f32),
-                    DMA((3,)),
-                ],
+                solve_scratch,
                 all_flops + solve_flops,
-                panel_bytes,
+                panel_bytes + arrived_bytes,
+                panel_bytes + arrived_bytes + 6 * column_bytes,
             )(panel, arrived, field, incident, self_inverse)
-            own, received, keeps = spread(current)
             field = call(
                 partial_kernel,
                 shape(column, f32),
@@ -278,8 +287,10 @@
                 HBM,
                 [pltpu.VMEM(column, f32), DMA],
                 all_flops,
-                panel_bytes,
+                panel_bytes + arrived_bytes,
+                panel_bytes + arrived_bytes + 4 * column_bytes,
             )(panel, arrived, field, current)
+            after = [field]
         else:
             field = call(
                 ahead_kernel,
@@ -288,9 +299,10 @@
                 VMEM,
                 [pltpu.VMEM(column, f32), DMA],
                 all_flops,
-                panel_bytes,
+                panel_bytes + arrived_bytes,
+                panel_bytes + arrived_bytes + 4 * column_bytes,
             )(panel, arrived, field)
-    return currents[0], field[None]
+    return currents, field[None]
 
 
 def solution(mesh):

time: 135 us -> 138 us (1.022); the launches traced: 134 us -> 135 us
  blocking collectives: 0 us -> 12.1 us
  local copies, waits for them, and re-layouts: 25.5 us -> 19 us
  starting transfers between devices: 39.2 us -> 36.1 us
    all_to_all x0 -> x1, blocking collectives: none -> 12.1 us  [exchange(): return lax.all_to_all(x, 'patch', split_axis=0, concat_axis=0, tiled=True)]
    unnamed x38, local copies, waits for them, and re-layouts: 25.5 us -> 19 us
    all_to_all x5 -> x4, starting transfers between devices: 22.6 us -> 16.7 us  [exchange(): return lax.all_to_all(x, 'patch', split_axis=0, concat_axis=0, tiled=True)]
    ppermute x4, waiting for transfers between devices: 9.02 us -> 3.95 us  [spread(): received = lax.ppermute(x, 'lag', pairs)]
    all_to_all x5 -> x4, waiting for transfers between devices: 7.34 us -> 10.8 us  [exchange(): return lax.all_to_all(x, 'patch', split_axis=0, concat_axis=0, tiled=True)]
    ppermute x4, starting transfers between devices: 11.3 us -> 14.1 us  [spread(): received = lax.ppermute(x, 'lag', pairs)]
    pallas_call x5 -> x9, Pallas kernels: 7.16 us -> 7.74 us  [the longest x8 7.16 us: pack(): call(lambda *refs: pack_kernel(step, keeps, early, *refs), (shape((patche...]
  transfers between devices with their start and end apart: 13 -> 12, of which waited for: 12 -> 11; matrix products, arithmetic and copies ran while one was open for 0% -> 0% of each run, Pallas kernels for 4% -> 7%
where the time goes in v1:
time: 138 us; the launch traced here: 135 us
  waiting for transfers between devices  47.9 us (35%)
  starting transfers between devices  36.1 us (26%)
  local copies, waits for them, and re-layouts  19 us (14%)
  Pallas kernels  19 us (14%)
  blocking collectives  12.1 us (9%)
    ppermute x4, waiting for transfers between devices, shifted(): return lax.ppermute(x, 'lag', [(i, i - 1) for i in range(1, sections)])  33.2 us
    unnamed x38, local copies, waits for them, and re-layouts  19 us
    all_to_all x4, starting transfers between devices, exchange(): return lax.all_to_all(x, 'patch', split_axis=0, concat_axis=0, tiled=True)  16.7 us
    ppermute x4, starting transfers between devices, spread(): received = lax.ppermute(x, 'lag', pairs)  14.1 us
    all_to_all x1, blocking collectives, exchange(): return lax.all_to_all(x, 'patch', split_axis=0, concat_axis=0, tiled=True)  12.1 us
    all_to_all x4, waiting for transfers between devices, exchange(): return lax.all_to_all(x, 'patch', split_axis=0, concat_axis=0, tiled=True)  10.8 us
    pallas_call x8, Pallas kernels, pack(): call(lambda *refs: pack_kernel(step, keeps, early, *refs), (shape((patche...  7.16 us
    pallas_call x3, Pallas kernels, body(): call(lambda *refs, n=step + 1: solve_kernel(n, *refs), shape(column, bf16...  5.66 us
  transfers between devices with their start and end apart: 12, of which 11 were waited for; matrix products, arithmetic and copies ran while one was open for 0% of the time, Pallas kernels for 7%

profile of v1, /device:TPU:0, one launch (start us, length us, event | category | flops | bytes accessed | tf_op | source)
XLA Modules:
  0.0 135.2 jit_solution(12557018420693329527)
XLA Ops:
  6.6 4.3 %collective-permute-start = (bf16[512,128]{1,0:T(8,128)(2,1)S(1)}, bf16[512,128]{1,0:T(8,128)(2,1)S(1)}, u32[]{:S(2)}, u32[]{:S(2)}) collective-permute-start(bf16[512,128]{1,0:T(8,128)(2,1)S(1)} %shard_map.88.refs_1_), channel_id=1, source_target_pairs={{0,16},{1,17},{2,18},{3,19},{4,20},{5,21},{6,22},{7,23},{8,24},{9,... | collective-permute-start | bytes 393224 | tf_op jit(solution)/shard_map/ppermute | solution.py:187
  10.9 12.1 %all_to_all.25.refs_0_ = s32[16,1,128]{2,1,0:T(1,128)S(1)} all-to-all(s32[16,1,128]{2,1,0:T(1,128)S(1)} %shard_map.86.after), channel_id=1, replica_groups=mesh['lag'=2,'patch'=16] {'patch'}, dimensions={0} | all-to-all | bytes 16384 | tf_op jit(solution)/shard_map/all_to_all | solution.py:207
  23.0 1.6 %shard_map.89 = (bf16[16,128,128]{2,1,0:T(8,128)(2,1)}, bf16[4,512,128]{2,1,0:T(8,128)(2,1)}) custom-call(s32[16,1,128]{2,1,0:T(1,128)S(1)} %all_to_all.25.refs_0_, bf16[512,128]{1,0:T(8,128)(2,1)S(1)} %shard_map.88.refs_1_), custom_call_target="tpu_custom_call" | custom-call | tf_op jit(solution)/shard_map/pallas_call | solution.py:216
  24.8 3.6 %all-to-all-start.1 = ((bf16[16,128,128]{2,1,0:T(8,128)(2,1)}), bf16[16,128,128]{2,1,0:T(8,128)(2,1)S(1)}, u32[]{:S(2)}, u32[]{:S(2)}) async-start(bf16[16,128,128]{2,1,0:T(8,128)(2,1)} %get-tuple-element.20), calls=%async_computation.1 | async-start | bytes 1048576 | tf_op jit(solution)/shard_map/all_to_all | solution.py:207
  28.4 1.4 %collective-permute-start.1 = (f32[512,128]{1,0:T(8,128)}, f32[512,128]{1,0:T(8,128)S(1)}, u32[]{:S(2)}, u32[]{:S(2)}) collective-permute-start(f32[512,128]{1,0:T(8,128)} %bitcast.2), channel_id=1, source_target_pairs={{16,0},{17,1},{18,2},{19,3},{20,4},{21,5},{22,6},{23,7},{24,8},{25... | collective-permute-start | bytes 786440 | tf_op jit(solution)/shard_map/ppermute | solution.py:176
  29.9 2.0 %copy-done.12 = f32[1,1,56,128,128]{4,3,2,1,0:T(8,128)S(1)} copy-done((f32[1,1,56,128,128]{4,3,2,1,0:T(8,128)S(1)}, f32[1,1,56,128,128]{4,3,2,1,0:T(8,128)}, u32[]{:S(2)}) %copy-start.12) | copy-done | bytes 3670040
  33.9 2.5 %shard_map.87.refs_0_.panel = bf16[2,512,2048]{2,1,0:T(8,128)(2,1)S(1)} custom-call(s32[1,1,56]{2,1,0:T(1,128)S(1)} %copy-done.18, s32[1,1,56]{2,1,0:T(1,128)S(1)} %copy-done.15, s32[64]{0:T(128)S(1)} %copy-done.17, f32[1,1,56,128,128]{4,3,2,1,0:T(8,128)S(1)} %copy-done.12), custom_call_target="tpu_custom_call" | custom-call | bytes 7864320 | tf_op jit(solution)/shard_map/pallas_call | solution.py:253
  36.4 2.0 %copy-done = bf16[2,512,2048]{2,1,0:T(8,128)(2,1)} copy-done((bf16[2,512,2048]{2,1,0:T(8,128)(2,1)}, bf16[2,512,2048]{2,1,0:T(8,128)(2,1)S(1)}, u32[]{:S(2)}) %copy-start) | copy-done | bytes 4194328
  39.2 3.7 %all-to-all-done.1.refs_1_.arrived = bf16[16,128,128]{2,1,0:T(8,128)(2,1)S(1)} async-done(((bf16[16,128,128]{2,1,0:T(8,128)(2,1)}), bf16[16,128,128]{2,1,0:T(8,128)(2,1)S(1)}, u32[]{:S(2)}, u32[]{:S(2)}) %all-to-all-start.1) | async-done | bytes 524320 | tf_op jit(solution)/shard_map/all_to_all | solution.py:207
  42.8 2.2 %copy-done.1 = bf16[2,512,2048]{2,1,0:T(8,128)(2,1)S(1)} copy-done((bf16[2,512,2048]{2,1,0:T(8,128)(2,1)S(1)}, bf16[2,512,2048]{2,1,0:T(8,128)(2,1)}, u32[]{:S(2)}) %copy-start.1) | copy-done | bytes 4194328
  45.0 1.9 %shard_map.91.after.refs_1_ = bf16[512,128]{1,0:T(8,128)(2,1)S(1)} custom-call(bf16[2,512,2048]{2,1,0:T(8,128)(2,1)S(1)} %copy-done.1, bf16[16,128,128]{2,1,0:T(8,128)(2,1)S(1)} %all-to-all-done.1.refs_1_.arrived, f32[512,128]{1,0:T(8,128)S(1)} %collective-permute-done.1.refs_2_.field_hbm, bf16[4,512,128]{2,1,0:T(8,128)(2,1)S(1)} %copy-done.9, ...), custom_call_target="tpu_custom_call" | custom-call | flops 637534208 | bytes 4718592 | tf_op jit(solution)/shard_map/pallas_call | solution.py:273
  48.2 1.6 %shard_map.93 = (bf16[16,128,128]{2,1,0:T(8,128)(2,1)}, bf16[4,512,128]{2,1,0:T(8,128)(2,1)}) custom-call(s32[16,1,128]{2,1,0:T(1,128)S(1)} %all_to_all.25.refs_0_, bf16[512,128]{1,0:T(8,128)(2,1)S(1)} %shard_map.91.after.refs_1_, bf16[4,512,128]{2,1,0:T(8,128)(2,1)} %get-tuple-element.21.refs_2_), custom_call_target="tpu_custom_call", output_to_operand_aliasing={{1}: (2, {})} | custom-call | tf_op jit(solution)/shard_map/pallas_call | solution.py:216
  49.9 1.5 %collective-permute-done.2.refs_1_ = bf16[512,128]{1,0:T(8,128)(2,1)S(1)} collective-permute-done((bf16[512,128]{1,0:T(8,128)(2,1)S(1)}, bf16[512,128]{1,0:T(8,128)(2,1)S(1)}, u32[]{:S(2)}, u32[]{:S(2)}) %collective-permute-start.2) | collective-permute-done | bytes 131104 | tf_op jit(solution)/shard_map/ppermute | solution.py:187
  51.6 4.3 %all-to-all-start.2 = ((bf16[16,128,128]{2,1,0:T(8,128)(2,1)}), bf16[16,128,128]{2,1,0:T(8,128)(2,1)S(1)}, u32[]{:S(2)}, u32[]{:S(2)}) async-start(bf16[16,128,128]{2,1,0:T(8,128)(2,1)} %get-tuple-element.24), calls=%async_computation.2 | async-start | bytes 1048576 | tf_op jit(solution)/shard_map/all_to_all | solution.py:207
  57.2 10.8 %collective-permute-done.3.refs_2_.field_hbm = f32[512,128]{1,0:T(8,128)S(1)} collective-permute-done((f32[512,128]{1,0:T(8,128)S(1)}, f32[512,128]{1,0:T(8,128)S(1)}, u32[]{:S(2)}, u32[]{:S(2)}) %collective-permute-start.3) | collective-permute-done | bytes 262176 | tf_op jit(solution)/shard_map/ppermute | solution.py:176
  68.0 2.4 %all-to-all-done.2.refs_1_.arrived = bf16[16,128,128]{2,1,0:T(8,128)(2,1)S(1)} async-done(((bf16[16,128,128]{2,1,0:T(8,128)(2,1)}), bf16[16,128,128]{2,1,0:T(8,128)(2,1)S(1)}, u32[]{:S(2)}, u32[]{:S(2)}) %all-to-all-start.2) | async-done | bytes 524320 | tf_op jit(solution)/shard_map/all_to_all | solution.py:207
  70.4 2.2 %copy-done.3 = bf16[2,512,2048]{2,1,0:T(8,128)(2,1)S(1)} copy-done((bf16[2,512,2048]{2,1,0:T(8,128)(2,1)S(1)}, bf16[2,512,2048]{2,1,0:T(8,128)(2,1)}, u32[]{:S(2)}) %copy-start.3) | copy-done | bytes 4194328
  72.6 1.9 %shard_map.95.after.refs_1_ = bf16[512,128]{1,0:T(8,128)(2,1)S(1)} custom-call(bf16[2,512,2048]{2,1,0:T(8,128)(2,1)S(1)} %copy-done.3, bf16[16,128,128]{2,1,0:T(8,128)(2,1)S(1)} %all-to-all-done.2.refs_1_.arrived, f32[512,128]{1,0:T(8,128)S(1)} %collective-permute-done.3.refs_2_.field_hbm, bf16[4,512,128]{2,1,0:T(8,128)(2,1)S(1)} %copy-done.9, ...), custom_call_target="tpu_custom_call" | custom-call | flops 637534208 | bytes 4718592 | tf_op jit(solution)/shard_map/pallas_call | solution.py:273
  74.5 4.3 %collective-permute-start.4 = (bf16[512,128]{1,0:T(8,128)(2,1)S(1)}, bf16[512,128]{1,0:T(8,128)(2,1)S(1)}, u32[]{:S(2)}, u32[]{:S(2)}) collective-permute-start(bf16[512,128]{1,0:T(8,128)(2,1)S(1)} %shard_map.95.after.refs_1_), channel_id=1, source_target_pairs={{0,16},{1,17},{2,18},{3,19},{4,20},{5,21},{6,22},{7,23},{8,24},{9,... | collective-permute-start | bytes 393224 | tf_op jit(solution)/shard_map/ppermute | solution.py:187
  78.7 1.6 %shard_map.97 = (bf16[16,128,128]{2,1,0:T(8,128)(2,1)}, bf16[4,512,128]{2,1,0:T(8,128)(2,1)}) custom-call(s32[16,1,128]{2,1,0:T(1,128)S(1)} %all_to_all.25.refs_0_, bf16[512,128]{1,0:T(8,128)(2,1)S(1)} %shard_map.95.after.refs_1_, bf16[4,512,128]{2,1,0:T(8,128)(2,1)} %get-tuple-element.25.refs_2_), custom_call_target="tpu_custom_call", output_to_operand_aliasing={{1}: (2, {})} | custom-call | tf_op jit(solution)/shard_map/pallas_call | solution.py:216
  81.8 4.4 %all-to-all-start.3 = ((bf16[16,128,128]{2,1,0:T(8,128)(2,1)}), bf16[16,128,128]{2,1,0:T(8,128)(2,1)S(1)}, u32[]{:S(2)}, u32[]{:S(2)}) async-start(bf16[16,128,128]{2,1,0:T(8,128)(2,1)} %get-tuple-element.28), calls=%async_computation.3 | async-start | bytes 1048576 | tf_op jit(solution)/shard_map/all_to_all | solution.py:207
  87.5 10.8 %collective-permute-done.5.refs_2_.field_hbm = f32[512,128]{1,0:T(8,128)S(1)} collective-permute-done((f32[512,128]{1,0:T(8,128)S(1)}, f32[512,128]{1,0:T(8,128)S(1)}, u32[]{:S(2)}, u32[]{:S(2)}) %collective-permute-start.5) | collective-permute-done | bytes 262176 | tf_op jit(solution)/shard_map/ppermute | solution.py:176
  98.3 2.4 %all-to-all-done.3.refs_1_.arrived = bf16[16,128,128]{2,1,0:T(8,128)(2,1)S(1)} async-done(((bf16[16,128,128]{2,1,0:T(8,128)(2,1)}), bf16[16,128,128]{2,1,0:T(8,128)(2,1)S(1)}, u32[]{:S(2)}, u32[]{:S(2)}) %all-to-all-start.3) | async-done | bytes 524320 | tf_op jit(solution)/shard_map/all_to_all | solution.py:207
  100.7 2.2 %copy-done.5 = bf16[2,512,2048]{2,1,0:T(8,128)(2,1)S(1)} copy-done((bf16[2,512,2048]{2,1,0:T(8,128)(2,1)S(1)}, bf16[2,512,2048]{2,1,0:T(8,128)(2,1)}, u32[]{:S(2)}) %copy-start.5) | copy-done | bytes 4194328
  102.9 1.9 %shard_map.99.after.refs_1_ = bf16[512,128]{1,0:T(8,128)(2,1)S(1)} custom-call(bf16[2,512,2048]{2,1,0:T(8,128)(2,1)S(1)} %copy-done.5, bf16[16,128,128]{2,1,0:T(8,128)(2,1)S(1)} %all-to-all-done.3.refs_1_.arrived, f32[512,128]{1,0:T(8,128)S(1)} %collective-permute-done.5.refs_2_.field_hbm, bf16[4,512,128]{2,1,0:T(8,128)(2,1)S(1)} %copy-done.9, ...), custom_call_target="tpu_custom_call" | custom-call | flops 637534208 | bytes 4718592 | tf_op jit(solution)/shard_map/pallas_call | solution.py:273
  104.8 4.3 %collective-permute-start.6 = (bf16[512,128]{1,0:T(8,128)(2,1)S(1)}, bf16[512,128]{1,0:T(8,128)(2,1)S(1)}, u32[]{:S(2)}, u32[]{:S(2)}) collective-permute-start(bf16[512,128]{1,0:T(8,128)(2,1)S(1)} %shard_map.99.after.refs_1_), channel_id=1, source_target_pairs={{0,16},{1,17},{2,18},{3,19},{4,20},{5,21},{6,22},{7,23},{8,24},{9,... | collective-permute-start | bytes 393224 | tf_op jit(solution)/shard_map/ppermute | solution.py:187
  109.0 1.6 %shard_map.101 = (bf16[16,128,128]{2,1,0:T(8,128)(2,1)}, bf16[4,512,128]{2,1,0:T(8,128)(2,1)}) custom-call(s32[16,1,128]{2,1,0:T(1,128)S(1)} %all_to_all.25.refs_0_, bf16[512,128]{1,0:T(8,128)(2,1)S(1)} %shard_map.99.after.refs_1_, bf16[4,512,128]{2,1,0:T(8,128)(2,1)} %get-tuple-element.29.refs_2_), custom_call_target="tpu_custom_call", output_to_operand_aliasing={{1}: (2, {})} | custom-call | tf_op jit(solution)/shard_map/pallas_call | solution.py:216
  112.1 4.4 %all-to-all-start.4 = ((bf16[16,128,128]{2,1,0:T(8,128)(2,1)}), bf16[16,128,128]{2,1,0:T(8,128)(2,1)S(1)}, u32[]{:S(2)}, u32[]{:S(2)}) async-start(bf16[16,128,128]{2,1,0:T(8,128)(2,1)} %get-tuple-element.33), calls=%async_computation.4 | async-start | bytes 1048576 | tf_op jit(solution)/shard_map/all_to_all | solution.py:207
  117.8 10.8 %collective-permute-done.7.field_hbm = f32[512,128]{1,0:T(8,128)S(1)} collective-permute-done((f32[512,128]{1,0:T(8,128)S(1)}, f32[512,128]{1,0:T(8,128)S(1)}, u32[]{:S(2)}, u32[]{:S(2)}) %collective-permute-start.7) | collective-permute-done | bytes 262176 | tf_op jit(solution)/shard_map/ppermute | solution.py:176
  128.6 2.4 %all-to-all-done.4.arrived = bf16[16,128,128]{2,1,0:T(8,128)(2,1)S(1)} async-done(((bf16[16,128,128]{2,1,0:T(8,128)(2,1)}), bf16[16,128,128]{2,1,0:T(8,128)(2,1)S(1)}, u32[]{:S(2)}, u32[]{:S(2)}) %all-to-all-start.4) | async-done | bytes 524320 | tf_op jit(solution)/shard_map/all_to_all | solution.py:207
  131.0 2.2 %copy-done.7 = bf16[2,512,2048]{2,1,0:T(8,128)(2,1)S(1)} copy-done((bf16[2,512,2048]{2,1,0:T(8,128)(2,1)S(1)}, bf16[2,512,2048]{2,1,0:T(8,128)(2,1)}, u32[]{:S(2)}) %copy-start.7) | copy-done | bytes 4194328
  133.2 2.0 %shard_map.103 = f32[512,128]{1,0:T(8,128)} custom-call(bf16[2,512,2048]{2,1,0:T(8,128)(2,1)S(1)} %copy-done.7, bf16[16,128,128]{2,1,0:T(8,128)(2,1)S(1)} %all-to-all-done.4.arrived, f32[512,128]{1,0:T(8,128)S(1)} %collective-permute-done.7.field_hbm), custom_call_target="tpu_custom_call" | custom-call | flops 536870912 | bytes 4718592 | tf_op jit(solution)/shard_map/pallas_call | solution.py:295
  (49 shorter events, 17.0 us)
Async XLA Ops:
  0.6 0.7 copy-start.14
  1.3 0.7 copy-start.16
  3.0 1.0 copy-start.8
  4.1 0.9 copy-start.10
  5.0 0.9 copy-start.13
  6.6 18.1 %collective-permute-start = (bf16[512,128]{1,0:T(8,128)(2,1)S(1)}, bf16[512,128]{1,0:T(8,128)(2,1)S(1)}, u32[]{:S(2)}, u32[]{:S(2)}) collective-permute-start(bf16[512,128]{1,0:T(8,128)(2,1)S(1)} %shard_map.88.refs_1_), channel_id=1, source_target_pairs={{0,16},{1,17},{2,18},{3,19},{4,20},{5,21},{6,22},{7,23},{8,24},{9,... | collective-permute-start | bytes 393224 | tf_op jit(solution)/shard_map/ppermute | solution.py:187
  24.8 18.0 %all-to-all-start.1 = ((bf16[16,128,128]{2,1,0:T(8,128)(2,1)}), bf16[16,128,128]{2,1,0:T(8,128)(2,1)S(1)}, u32[]{:S(2)}, u32[]{:S(2)}) async-start(bf16[16,128,128]{2,1,0:T(8,128)(2,1)} %get-tuple-element.20), calls=%async_computation.1 | async-start | bytes 1048576 | tf_op jit(solution)/shard_map/all_to_all | solution.py:207
  28.4 14.4 %copy-start.9 = (bf16[4,512,128]{2,1,0:T(8,128)(2,1)S(1)}, bf16[4,512,128]{2,1,0:T(8,128)(2,1)}, u32[]{:S(2)}) copy-start(bf16[4,512,128]{2,1,0:T(8,128)(2,1)} %refs_3_.7) | copy-start | bytes 1572868
  28.4 14.4 %copy-start.11 = (f32[4,128,128]{2,1,0:T(8,128)S(1)}, f32[4,128,128]{2,1,0:T(8,128)}, u32[]{:S(2)}) copy-start(f32[4,128,128]{2,1,0:T(8,128)} %refs_4_.5) | copy-start | bytes 786436
  28.4 10.7 %collective-permute-start.1 = (f32[512,128]{1,0:T(8,128)}, f32[512,128]{1,0:T(8,128)S(1)}, u32[]{:S(2)}, u32[]{:S(2)}) collective-permute-start(f32[512,128]{1,0:T(8,128)} %bitcast.2), channel_id=1, source_target_pairs={{16,0},{17,1},{18,2},{19,3},{20,4},{21,5},{22,6},{23,7},{24,8},{25... | collective-permute-start | bytes 786440 | tf_op jit(solution)/shard_map/ppermute | solution.py:176
  29.9 2.0 %copy-start.12 = (f32[1,1,56,128,128]{4,3,2,1,0:T(8,128)S(1)}, f32[1,1,56,128,128]{4,3,2,1,0:T(8,128)}, u32[]{:S(2)}) copy-start(f32[1,1,56,128,128]{4,3,2,1,0:T(8,128)} %refs_3_.4) | copy-start | bytes 11010052
  31.9 0.7 copy-start.15
  32.6 0.7 copy-start.17
  33.2 0.7 copy-start.18
  36.4 2.0 %copy-start = (bf16[2,512,2048]{2,1,0:T(8,128)(2,1)}, bf16[2,512,2048]{2,1,0:T(8,128)(2,1)S(1)}, u32[]{:S(2)}) copy-start(bf16[2,512,2048]{2,1,0:T(8,128)(2,1)S(1)} %shard_map.87.refs_0_.panel) | copy-start | bytes 12582916
  42.8 2.2 %copy-start.1 = (bf16[2,512,2048]{2,1,0:T(8,128)(2,1)S(1)}, bf16[2,512,2048]{2,1,0:T(8,128)(2,1)}, u32[]{:S(2)}) copy-start(bf16[2,512,2048]{2,1,0:T(8,128)(2,1)} %copy-done) | copy-start | bytes 12582916
  45.0 4.8 %copy-start.2 = (bf16[2,512,2048]{2,1,0:T(8,128)(2,1)S(1)}, bf16[2,512,2048]{2,1,0:T(8,128)(2,1)}, u32[]{:S(2)}) copy-start(bf16[2,512,2048]{2,1,0:T(8,128)(2,1)} %copy-done) | copy-start | bytes 12582916
  46.9 4.5 %collective-permute-start.2 = (bf16[512,128]{1,0:T(8,128)(2,1)S(1)}, bf16[512,128]{1,0:T(8,128)(2,1)S(1)}, u32[]{:S(2)}, u32[]{:S(2)}) collective-permute-start(bf16[512,128]{1,0:T(8,128)(2,1)S(1)} %shard_map.91.after.refs_1_), channel_id=1, source_target_pairs={{0,16},{1,17},{2,18},{3,19},{4,20},{5,21},{6,22},{7,23},{8,24},{9,... | collective-permute-start | bytes 393224 | tf_op jit(solution)/shard_map/ppermute | solution.py:187
  51.6 18.8 %all-to-all-start.2 = ((bf16[16,128,128]{2,1,0:T(8,128)(2,1)}), bf16[16,128,128]{2,1,0:T(8,128)(2,1)S(1)}, u32[]{:S(2)}, u32[]{:S(2)}) async-start(bf16[16,128,128]{2,1,0:T(8,128)(2,1)} %get-tuple-element.24), calls=%async_computation.2 | async-start | bytes 1048576 | tf_op jit(solution)/shard_map/all_to_all | solution.py:207
  55.9 12.1 %collective-permute-start.3 = (f32[512,128]{1,0:T(8,128)S(1)}, f32[512,128]{1,0:T(8,128)S(1)}, u32[]{:S(2)}, u32[]{:S(2)}) collective-permute-start(f32[512,128]{1,0:T(8,128)S(1)} %shard_map.92.refs_2_), channel_id=1, source_target_pairs={{16,0},{17,1},{18,2},{19,3},{20,4},{21,5},{22,6},{23,7},{24,8},{25... | collective-permute-start | bytes 786440 | tf_op jit(solution)/shard_map/ppermute | solution.py:176
  70.4 2.2 %copy-start.3 = (bf16[2,512,2048]{2,1,0:T(8,128)(2,1)S(1)}, bf16[2,512,2048]{2,1,0:T(8,128)(2,1)}, u32[]{:S(2)}) copy-start(bf16[2,512,2048]{2,1,0:T(8,128)(2,1)} %copy-done) | copy-start | bytes 12582916
  72.6 7.8 %copy-start.4 = (bf16[2,512,2048]{2,1,0:T(8,128)(2,1)S(1)}, bf16[2,512,2048]{2,1,0:T(8,128)(2,1)}, u32[]{:S(2)}) copy-start(bf16[2,512,2048]{2,1,0:T(8,128)(2,1)} %copy-done) | copy-start | bytes 12582916
  74.5 7.2 %collective-permute-start.4 = (bf16[512,128]{1,0:T(8,128)(2,1)S(1)}, bf16[512,128]{1,0:T(8,128)(2,1)S(1)}, u32[]{:S(2)}, u32[]{:S(2)}) collective-permute-start(bf16[512,128]{1,0:T(8,128)(2,1)S(1)} %shard_map.95.after.refs_1_), channel_id=1, source_target_pairs={{0,16},{1,17},{2,18},{3,19},{4,20},{5,21},{6,22},{7,23},{8,24},{9,... | collective-permute-start | bytes 393224 | tf_op jit(solution)/shard_map/ppermute | solution.py:187
  81.8 18.9 %all-to-all-start.3 = ((bf16[16,128,128]{2,1,0:T(8,128)(2,1)}), bf16[16,128,128]{2,1,0:T(8,128)(2,1)S(1)}, u32[]{:S(2)}, u32[]{:S(2)}) async-start(bf16[16,128,128]{2,1,0:T(8,128)(2,1)} %get-tuple-element.28), calls=%async_computation.3 | async-start | bytes 1048576 | tf_op jit(solution)/shard_map/all_to_all | solution.py:207
  86.2 12.1 %collective-permute-start.5 = (f32[512,128]{1,0:T(8,128)S(1)}, f32[512,128]{1,0:T(8,128)S(1)}, u32[]{:S(2)}, u32[]{:S(2)}) collective-permute-start(f32[512,128]{1,0:T(8,128)S(1)} %shard_map.96.refs_2_), channel_id=1, source_target_pairs={{16,0},{17,1},{18,2},{19,3},{20,4},{21,5},{22,6},{23,7},{24,8},{25... | collective-permute-start | bytes 786440 | tf_op jit(solution)/shard_map/ppermute | solution.py:176
  100.7 2.2 %copy-start.5 = (bf16[2,512,2048]{2,1,0:T(8,128)(2,1)S(1)}, bf16[2,512,2048]{2,1,0:T(8,128)(2,1)}, u32[]{:S(2)}) copy-start(bf16[2,512,2048]{2,1,0:T(8,128)(2,1)} %copy-done) | copy-start | bytes 12582916
  102.9 7.8 %copy-start.6 = (bf16[2,512,2048]{2,1,0:T(8,128)(2,1)S(1)}, bf16[2,512,2048]{2,1,0:T(8,128)(2,1)}, u32[]{:S(2)}) copy-start(bf16[2,512,2048]{2,1,0:T(8,128)(2,1)} %copy-done) | copy-start | bytes 12582916
  104.8 7.2 %collective-permute-start.6 = (bf16[512,128]{1,0:T(8,128)(2,1)S(1)}, bf16[512,128]{1,0:T(8,128)(2,1)S(1)}, u32[]{:S(2)}, u32[]{:S(2)}) collective-permute-start(bf16[512,128]{1,0:T(8,128)(2,1)S(1)} %shard_map.99.after.refs_1_), channel_id=1, source_target_pairs={{0,16},{1,17},{2,18},{3,19},{4,20},{5,21},{6,22},{7,23},{8,24},{9,... | collective-permute-start | bytes 393224 | tf_op jit(solution)/shard_map/ppermute | solution.py:187
  112.1 18.9 %all-to-all-start.4 = ((bf16[16,128,128]{2,1,0:T(8,128)(2,1)}), bf16[16,128,128]{2,1,0:T(8,128)(2,1)S(1)}, u32[]{:S(2)}, u32[]{:S(2)}) async-start(bf16[16,128,128]{2,1,0:T(8,128)(2,1)} %get-tuple-element.33), calls=%async_computation.4 | async-start | bytes 1048576 | tf_op jit(solution)/shard_map/all_to_all | solution.py:207
  116.5 12.1 %collective-permute-start.7 = (f32[512,128]{1,0:T(8,128)S(1)}, f32[512,128]{1,0:T(8,128)S(1)}, u32[]{:S(2)}, u32[]{:S(2)}) collective-permute-start(f32[512,128]{1,0:T(8,128)S(1)} %shard_map.100.refs_2_), channel_id=1, source_target_pairs={{16,0},{17,1},{18,2},{19,3},{20,4},{21,5},{22,6},{23,7},{24,8},{25... | collective-permute-start | bytes 786440 | tf_op jit(solution)/shard_map/ppermute | solution.py:176
  131.0 2.2 %copy-start.7 = (bf16[2,512,2048]{2,1,0:T(8,128)(2,1)S(1)}, bf16[2,512,2048]{2,1,0:T(8,128)(2,1)}, u32[]{:S(2)}) copy-start(bf16[2,512,2048]{2,1,0:T(8,128)(2,1)} %copy-done) | copy-start | bytes 12582916
